TPU v7x, 128 devices: a whole 4x4x4 slice. The times are simulated.
128 devices in a mesh: section: 8 (over z, core), dp: 16 (over y, x).
Axes of the slice: x: 4, y: 4, z: 4, core: 2. Of those that a mesh axis runs over, the one named last changes fastest.
Arguments:
- step_rows: bfloat16 [3, 16, 16, 8192], P(None, None, 'dp'), may hold values from -6 to 6
- cache: bfloat16 [8, 16, 16, 32, 2048], P('section', None, 'dp'), may hold values from -400 to 400
- new_kv: bfloat16 [8, 3, 16, 16, 2048], P('section', None, None, 'dp'), may hold values from -6 to 6
- gains: bfloat16 [8, 8192], P('section'), may hold values from 0.25 to 1.75
- parents: int32 [3, 16, 16, 1], replicated, may hold values from 0 to 15; in each aligned block of 8 rows (0 to 7, 8 to 15, ..., all dimensions but the last counted through in order) no two rows name the same one
Outputs:
- layer_rows: bfloat16 [8, 3, 16, 16, 8192], P('section', None, None, 'dp')
- cache_out: bfloat16 [8, 16, 16, 32, 2048], P('section', None, 'dp')
Inputs may be any that keep to these rules, and one draw needn't show every extreme that they name: Within each aligned block of 8 requests, the parents of one beam at one step are distinct beams.
All inputs are finite; a program needn't handle non-finite values.
Results may differ from a plain program's by a relative error of at most 0.02.
Values may be sent and summed in bfloat16 or wider, within the bound.
No kernel may reach another device: no remote copies, remote signals or barrier semaphores. Data moves between devices by JAX's collectives and lax.ppermute only.
A program may use at most 64 MiB of HBM per device.

v0:
```python
import jax
import jax.numpy as jnp
from jax import lax
from jax.sharding import PartitionSpec as P

HEADS = 64
KVH = 8
HD = 128


def from_behind(block, axis, distance):
    devices = range(lax.axis_size(axis))
    route = [(i - distance, i) for i in devices if i - distance in devices]
    return lax.ppermute(block, axis, route)


def attend(rows, slots, gain, pos):
    group = rows.shape[0]
    length = slots.shape[1]
    x = rows.astype(jnp.float32)
    scale = lax.rsqrt(jnp.mean(x * x, axis=-1, keepdims=True) + 1e-05)
    query = (x * scale * gain.astype(jnp.float32)).astype(jnp.bfloat16)
    query = query.reshape(group, KVH, HEADS // KVH, HD)
    keys = slots[:, :, : KVH * HD].reshape(group, length, KVH, HD)
    values = slots[:, :, KVH * HD :].reshape(group, length, KVH, HD)
    scores = jnp.einsum(
        "rkgd,rlkd->rkgl", query, keys, preferred_element_type=jnp.float32
    ) * HD ** (-0.5)
    live = jnp.arange(length) <= pos
    scores = jnp.where(live, scores, -1e30)
    top = jnp.max(scores, axis=-1, keepdims=True)
    expo = jnp.exp(scores - top)
    weights = (expo / jnp.sum(expo, axis=-1, keepdims=True)).astype(jnp.bfloat16)
    attended = jnp.einsum("rkgl,rlkd->rkgd", weights, values, preferred_element_type=jnp.float32)
    return (x + attended.reshape(group, HEADS * HD)).astype(jnp.bfloat16)


def outgoing_slots(older, chosen, mine, capacity):
    beams, group = chosen.shape
    match = (chosen == mine).astype(jnp.int32)
    ranks = jnp.cumsum(match, axis=1) - 1
    places = jnp.arange(capacity, dtype=jnp.int32)
    picks = (match[:, None, :] == 1) & (ranks[:, None, :] == places[None, :, None])
    having = jnp.any(picks, axis=2)
    which = jnp.sum(
        picks.astype(jnp.int32) * jnp.arange(group, dtype=jnp.int32)[None, None, :], axis=2
    )
    return jnp.where(having[:, :, None, None], older[which], jnp.zeros((), older.dtype))


def place_arrived(arrived, chosen, mine, capacity):
    beams, group = chosen.shape
    sources = lax.dynamic_slice_in_dim(chosen, mine, 1, 0)[0]
    order = jnp.arange(group, dtype=jnp.int32)
    before = (sources[:, None] == sources[None, :]) & (order[None, :] < order[:, None])
    slot_rank = jnp.sum(before.astype(jnp.int32), axis=1)
    flat = arrived.reshape((beams * capacity,) + arrived.shape[2:])
    return flat[sources * capacity + slot_rank]


def on_device(step_rows, cache, new_kv, gains, parents):
    sections = lax.axis_size("section")
    mine = lax.axis_index("dp")
    section_now = lax.axis_index("section")
    steps = step_rows.shape[0]
    requests = cache.shape[1]
    length = cache.shape[3]
    features = cache.shape[4]
    width = step_rows.shape[3]
    start = length - steps
    slots = cache[0, :, 0]
    fresh = new_kv[0, :, :, 0]
    inputs = step_rows[:, :, 0]
    gain = gains[0]
    table = parents[:, :, :, 0]
    capacity = requests // 8
    states = []
    for step in range(steps):
        chosen = table[step]
        sending = outgoing_slots(slots, chosen, mine, capacity)
        arrived = lax.all_to_all(sending, "dp", split_axis=0, concat_axis=0, tiled=True)
        moved = place_arrived(arrived, chosen, mine, capacity)
        moved = moved.at[:, start + step].set(fresh[step])
        states.append(moved)
        slots = moved
    states = jnp.stack(states)
    blocks = requests // requests
    total = steps * blocks
    ticks = total + sections - 1

    def tick(index, carry):
        record, inflow = carry
        item = index - section_now
        valid = (item >= 0) & (item < total)
        clamped = jnp.clip(item, 0, total - 1)
        step = clamped // blocks
        first = clamped % blocks * requests
        block_slots = lax.dynamic_slice(
            states, (step, first, 0, 0), (1, requests, length, features)
        )[0]
        pos = start + step
        given = lax.dynamic_slice(inputs, (step, first, 0), (1, requests, width))[0]
        rows = jnp.where(section_now == 0, given, inflow)
        result = attend(rows, block_slots, gain, pos)
        prior = lax.dynamic_slice(record, (step, first, 0), (1, requests, width))
        record = lax.dynamic_update_slice(
            record, jnp.where(valid, result[None], prior), (step, first, 0)
        )
        inflow = from_behind(result, "section", 1)
        return (record, inflow)

    record = jnp.zeros((steps, requests, width), jnp.bfloat16)
    inflow = jnp.zeros((requests, width), jnp.bfloat16)
    record, inflow = lax.fori_loop(0, ticks, tick, (record, inflow))
    return (record[None, :, :, None], slots[None, :, None])


def solution(mesh):
    return jax.shard_map(
        on_device,
        mesh=mesh,
        in_specs=(
            P(None, None, "dp", None),
            P("section", None, "dp", None, None),
            P("section", None, None, "dp", None),
            P("section", None),
            P(),
        ),
        out_specs=(P("section", None, None, "dp", None), P("section", None, "dp", None, None)),
        check_vma=False,
    )
```

profile of v0, /device:TPU:96, one launch (start us, length us, event | category | flops | bytes accessed | tf_op | source)
XLA Modules:
  0.0 471.5 jit_solution(14286310436390595970)
XLA Ops:
  5.0 4.5 broadcast_select_fusion.2
  9.5 7.2 %all-to-all-start = ((bf16[16,2,32,2048]{3,2,1,0:T(8,128)(2,1)}), bf16[16,2,32,2048]{3,2,1,0:T(8,128)(2,1)}, u32[]{:S(2)}, u32[]{:S(2)}) async-start(bf16[16,2,32,2048]{3,2,1,0:T(8,128)(2,1)} %broadcast_select_fusion.2), calls=%async_computation | async-start | bytes 8388608 | tf_op jit(solution)/shard_map/all_to_all | solution.py:81
  18.1 61.8 %all-to-all-done = bf16[16,2,32,2048]{3,2,1,0:T(8,128)(2,1)} async-done(((bf16[16,2,32,2048]{3,2,1,0:T(8,128)(2,1)}), bf16[16,2,32,2048]{3,2,1,0:T(8,128)(2,1)}, u32[]{:S(2)}, u32[]{:S(2)}) %all-to-all-start) | async-done | bytes 4194336 | tf_op jit(solution)/shard_map/all_to_all | solution.py:81
  80.0 4.3 gather_fusion.1
  87.6 4.3 gather_fusion.2
  91.9 4.5 broadcast_select_fusion.1
  96.4 4.6 all-to-all-start.1
  101.8 59.6 %all-to-all-done.1 = bf16[16,2,32,2048]{3,2,1,0:T(8,128)(2,1)} async-done(((bf16[16,2,32,2048]{3,2,1,0:T(8,128)(2,1)}), bf16[16,2,32,2048]{3,2,1,0:T(8,128)(2,1)}, u32[]{:S(2)}, u32[]{:S(2)}) %all-to-all-start.1) | async-done | bytes 4194336 | tf_op jit(solution)/shard_map/all_to_all | solution.py:81
  169.0 4.4 gather_fusion.4
  173.3 4.5 broadcast_select_fusion
  177.8 4.7 all-to-all-start.2
  182.9 57.1 %all-to-all-done.2 = bf16[16,2,32,2048]{3,2,1,0:T(8,128)(2,1)} async-done(((bf16[16,2,32,2048]{3,2,1,0:T(8,128)(2,1)}), bf16[16,2,32,2048]{3,2,1,0:T(8,128)(2,1)}, u32[]{:S(2)}, u32[]{:S(2)}) %all-to-all-start.2) | async-done | bytes 4194336 | tf_op jit(solution)/shard_map/all_to_all | solution.py:81
  247.6 6.2 %pad_maximum_fusion = bf16[3,16,32,2048]{3,2,1,0:T(8,128)(2,1)} fusion(bf16[1,16,32,2048]{3,2,1,0:T(8,128)(2,1)} %bitcast.133, bf16[1,16,32,2048]{3,2,1,0:T(8,128)(2,1)} %bitcast.126, bf16[1,16,32,2048]{3,2,1,0:T(8,128)(2,1)} %bitcast.127), kind=kLoop, calls=%fused_computation.34 | loop fusion | flops 6291456 | bytes 12582912 | tf_op jit(solution)/shard_map/stack | solution.py:86
  255.5 216.0 %while.20 = (s32[]{:T(128)}, bf16[3,16,8192]{2,1,0:T(8,128)(2,1)}, bf16[16,8192]{1,0:T(8,128)(2,1)}, s32[]{:T(128)}, pred[]{:T(512)}, /*index=5*/bf16[3,16,8192]...) while((s32[]{:T(128)}, bf16[3,16,8192]{2,1,0:T(8,128)(2,1)}, ...), condition=%wide.region_16.17_spmd, body=%wide.region_12.0_spmd.sunk | while | flops 18588792 | bytes 18834064 | solution.py:114
  270.6 5.8 %collective-permute-done = bf16[16,8192]{1,0:T(8,128)(2,1)S(1)} collective-permute-done((bf16[16,8192]{1,0:T(8,128)(2,1)S(1)}, bf16[16,8192]{1,0:T(8,128)(2,1)S(1)}, u32[]{:S(2)}, u32[]{:S(2)}) %collective-permute-start) | collective-permute-done | bytes 262176 | tf_op jit(solution)/shard_map/while/body/eval_jaxpr/ppermute | solution.py:14
  292.2 5.8 %collective-permute-done = bf16[16,8192]{1,0:T(8,128)(2,1)S(1)} collective-permute-done((bf16[16,8192]{1,0:T(8,128)(2,1)S(1)}, bf16[16,8192]{1,0:T(8,128)(2,1)S(1)}, u32[]{:S(2)}, u32[]{:S(2)}) %collective-permute-start) | collective-permute-done | bytes 262176 | tf_op jit(solution)/shard_map/while/body/eval_jaxpr/ppermute | solution.py:14
  313.8 5.8 %collective-permute-done = bf16[16,8192]{1,0:T(8,128)(2,1)S(1)} collective-permute-done((bf16[16,8192]{1,0:T(8,128)(2,1)S(1)}, bf16[16,8192]{1,0:T(8,128)(2,1)S(1)}, u32[]{:S(2)}, u32[]{:S(2)}) %collective-permute-start) | collective-permute-done | bytes 262176 | tf_op jit(solution)/shard_map/while/body/eval_jaxpr/ppermute | solution.py:14
  335.4 5.8 %collective-permute-done = bf16[16,8192]{1,0:T(8,128)(2,1)S(1)} collective-permute-done((bf16[16,8192]{1,0:T(8,128)(2,1)S(1)}, bf16[16,8192]{1,0:T(8,128)(2,1)S(1)}, u32[]{:S(2)}, u32[]{:S(2)}) %collective-permute-start) | collective-permute-done | bytes 262176 | tf_op jit(solution)/shard_map/while/body/eval_jaxpr/ppermute | solution.py:14
  357.0 5.8 %collective-permute-done = bf16[16,8192]{1,0:T(8,128)(2,1)S(1)} collective-permute-done((bf16[16,8192]{1,0:T(8,128)(2,1)S(1)}, bf16[16,8192]{1,0:T(8,128)(2,1)S(1)}, u32[]{:S(2)}, u32[]{:S(2)}) %collective-permute-start) | collective-permute-done | bytes 262176 | tf_op jit(solution)/shard_map/while/body/eval_jaxpr/ppermute | solution.py:14
  378.6 5.8 %collective-permute-done = bf16[16,8192]{1,0:T(8,128)(2,1)S(1)} collective-permute-done((bf16[16,8192]{1,0:T(8,128)(2,1)S(1)}, bf16[16,8192]{1,0:T(8,128)(2,1)S(1)}, u32[]{:S(2)}, u32[]{:S(2)}) %collective-permute-start) | collective-permute-done | bytes 262176 | tf_op jit(solution)/shard_map/while/body/eval_jaxpr/ppermute | solution.py:14
  400.2 5.8 %collective-permute-done = bf16[16,8192]{1,0:T(8,128)(2,1)S(1)} collective-permute-done((bf16[16,8192]{1,0:T(8,128)(2,1)S(1)}, bf16[16,8192]{1,0:T(8,128)(2,1)S(1)}, u32[]{:S(2)}, u32[]{:S(2)}) %collective-permute-start) | collective-permute-done | bytes 262176 | tf_op jit(solution)/shard_map/while/body/eval_jaxpr/ppermute | solution.py:14
  421.8 5.8 %collective-permute-done = bf16[16,8192]{1,0:T(8,128)(2,1)S(1)} collective-permute-done((bf16[16,8192]{1,0:T(8,128)(2,1)S(1)}, bf16[16,8192]{1,0:T(8,128)(2,1)S(1)}, u32[]{:S(2)}, u32[]{:S(2)}) %collective-permute-start) | collective-permute-done | bytes 262176 | tf_op jit(solution)/shard_map/while/body/eval_jaxpr/ppermute | solution.py:14
  443.4 5.8 %collective-permute-done = bf16[16,8192]{1,0:T(8,128)(2,1)S(1)} collective-permute-done((bf16[16,8192]{1,0:T(8,128)(2,1)S(1)}, bf16[16,8192]{1,0:T(8,128)(2,1)S(1)}, u32[]{:S(2)}, u32[]{:S(2)}) %collective-permute-start) | collective-permute-done | bytes 262176 | tf_op jit(solution)/shard_map/while/body/eval_jaxpr/ppermute | solution.py:14
  465.0 5.8 %collective-permute-done = bf16[16,8192]{1,0:T(8,128)(2,1)S(1)} collective-permute-done((bf16[16,8192]{1,0:T(8,128)(2,1)S(1)}, bf16[16,8192]{1,0:T(8,128)(2,1)S(1)}, u32[]{:S(2)}, u32[]{:S(2)}) %collective-permute-start) | collective-permute-done | bytes 262176 | tf_op jit(solution)/shard_map/while/body/eval_jaxpr/ppermute | solution.py:14
  (255 shorter events, 184.9 us)
Async XLA Ops:
  9.5 7.2 %copy-start.4 = (bf16[1,3,16,1,2048]{4,2,3,1,0:T(8,128)(2,1)S(1)}, bf16[1,3,16,1,2048]{4,2,3,1,0:T(8,128)(2,1)}, u32[]{:S(2)}) copy-start(bf16[1,3,16,1,2048]{4,2,3,1,0:T(8,128)(2,1)} %param.15) | copy-start | bytes 589828
  9.5 7.4 %copy-start.5 = (s32[3,16,16,1]{2,3,1,0:T(1,128)S(1)}, s32[3,16,16,1]{2,3,1,0:T(1,128)}, u32[]{:S(2)}) copy-start(s32[3,16,16,1]{2,3,1,0:T(1,128)} %param.17) | copy-start | bytes 9220
  9.5 70.5 %all-to-all-start = ((bf16[16,2,32,2048]{3,2,1,0:T(8,128)(2,1)}), bf16[16,2,32,2048]{3,2,1,0:T(8,128)(2,1)}, u32[]{:S(2)}, u32[]{:S(2)}) async-start(bf16[16,2,32,2048]{3,2,1,0:T(8,128)(2,1)} %broadcast_select_fusion.2), calls=%async_computation | async-start | bytes 8388608 | tf_op jit(solution)/shard_map/all_to_all | solution.py:81
  96.4 65.0 %all-to-all-start.1 = ((bf16[16,2,32,2048]{3,2,1,0:T(8,128)(2,1)}), bf16[16,2,32,2048]{3,2,1,0:T(8,128)(2,1)}, u32[]{:S(2)}, u32[]{:S(2)}) async-start(bf16[16,2,32,2048]{3,2,1,0:T(8,128)(2,1)} %broadcast_select_fusion.1), calls=%async_computation.1 | async-start | bytes 8388608 | tf_op jit(solution)/shard_map/all_to_all | solution.py:81
  177.8 4.8 %copy-start.6 = (bf16[1,8192]{1,0:T(2,128)(2,1)S(1)}, bf16[1,8192]{1,0:T(2,128)(2,1)}, u32[]{:S(2)}) copy-start(bf16[1,8192]{1,0:T(2,128)(2,1)} %param.16) | copy-start | bytes 49156
  177.8 62.2 %all-to-all-start.2 = ((bf16[16,2,32,2048]{3,2,1,0:T(8,128)(2,1)}), bf16[16,2,32,2048]{3,2,1,0:T(8,128)(2,1)}, u32[]{:S(2)}, u32[]{:S(2)}) async-start(bf16[16,2,32,2048]{3,2,1,0:T(8,128)(2,1)} %broadcast_select_fusion), calls=%async_computation.2 | async-start | bytes 8388608 | tf_op jit(solution)/shard_map/all_to_all | solution.py:81
  255.5 3.0 copy-start.2
  268.7 7.7 %collective-permute-start = (bf16[16,8192]{1,0:T(8,128)(2,1)S(1)}, bf16[16,8192]{1,0:T(8,128)(2,1)S(1)}, u32[]{:S(2)}, u32[]{:S(2)}) collective-permute-start(bf16[16,8192]{1,0:T(8,128)(2,1)S(1)} %get-tuple-element.318), channel_id=1, source_target_pairs={{0,16},{16,32},{32,48},{48,64},{64,80},{80,96},{96,112},{1,17},{17... | collective-permute-start | bytes 786440 | tf_op jit(solution)/shard_map/while/body/eval_jaxpr/ppermute | solution.py:14
  277.1 3.0 copy-start.2
  290.3 7.7 %collective-permute-start = (bf16[16,8192]{1,0:T(8,128)(2,1)S(1)}, bf16[16,8192]{1,0:T(8,128)(2,1)S(1)}, u32[]{:S(2)}, u32[]{:S(2)}) collective-permute-start(bf16[16,8192]{1,0:T(8,128)(2,1)S(1)} %get-tuple-element.318), channel_id=1, source_target_pairs={{0,16},{16,32},{32,48},{48,64},{64,80},{80,96},{96,112},{1,17},{17... | collective-permute-start | bytes 786440 | tf_op jit(solution)/shard_map/while/body/eval_jaxpr/ppermute | solution.py:14
  298.7 3.0 copy-start.2
  311.9 7.7 %collective-permute-start = (bf16[16,8192]{1,0:T(8,128)(2,1)S(1)}, bf16[16,8192]{1,0:T(8,128)(2,1)S(1)}, u32[]{:S(2)}, u32[]{:S(2)}) collective-permute-start(bf16[16,8192]{1,0:T(8,128)(2,1)S(1)} %get-tuple-element.318), channel_id=1, source_target_pairs={{0,16},{16,32},{32,48},{48,64},{64,80},{80,96},{96,112},{1,17},{17... | collective-permute-start | bytes 786440 | tf_op jit(solution)/shard_map/while/body/eval_jaxpr/ppermute | solution.py:14
  320.3 3.0 copy-start.2
  333.5 7.7 %collective-permute-start = (bf16[16,8192]{1,0:T(8,128)(2,1)S(1)}, bf16[16,8192]{1,0:T(8,128)(2,1)S(1)}, u32[]{:S(2)}, u32[]{:S(2)}) collective-permute-start(bf16[16,8192]{1,0:T(8,128)(2,1)S(1)} %get-tuple-element.318), channel_id=1, source_target_pairs={{0,16},{16,32},{32,48},{48,64},{64,80},{80,96},{96,112},{1,17},{17... | collective-permute-start | bytes 786440 | tf_op jit(solution)/shard_map/while/body/eval_jaxpr/ppermute | solution.py:14
  341.9 3.0 copy-start.2
  355.1 7.7 %collective-permute-start = (bf16[16,8192]{1,0:T(8,128)(2,1)S(1)}, bf16[16,8192]{1,0:T(8,128)(2,1)S(1)}, u32[]{:S(2)}, u32[]{:S(2)}) collective-permute-start(bf16[16,8192]{1,0:T(8,128)(2,1)S(1)} %get-tuple-element.318), channel_id=1, source_target_pairs={{0,16},{16,32},{32,48},{48,64},{64,80},{80,96},{96,112},{1,17},{17... | collective-permute-start | bytes 786440 | tf_op jit(solution)/shard_map/while/body/eval_jaxpr/ppermute | solution.py:14
  363.5 3.0 copy-start.2
  376.7 7.7 %collective-permute-start = (bf16[16,8192]{1,0:T(8,128)(2,1)S(1)}, bf16[16,8192]{1,0:T(8,128)(2,1)S(1)}, u32[]{:S(2)}, u32[]{:S(2)}) collective-permute-start(bf16[16,8192]{1,0:T(8,128)(2,1)S(1)} %get-tuple-element.318), channel_id=1, source_target_pairs={{0,16},{16,32},{32,48},{48,64},{64,80},{80,96},{96,112},{1,17},{17... | collective-permute-start | bytes 786440 | tf_op jit(solution)/shard_map/while/body/eval_jaxpr/ppermute | solution.py:14
  385.1 3.0 copy-start.2
  398.3 7.7 %collective-permute-start = (bf16[16,8192]{1,0:T(8,128)(2,1)S(1)}, bf16[16,8192]{1,0:T(8,128)(2,1)S(1)}, u32[]{:S(2)}, u32[]{:S(2)}) collective-permute-start(bf16[16,8192]{1,0:T(8,128)(2,1)S(1)} %get-tuple-element.318), channel_id=1, source_target_pairs={{0,16},{16,32},{32,48},{48,64},{64,80},{80,96},{96,112},{1,17},{17... | collective-permute-start | bytes 786440 | tf_op jit(solution)/shard_map/while/body/eval_jaxpr/ppermute | solution.py:14
  406.7 3.0 copy-start.2
  419.9 7.7 %collective-permute-start = (bf16[16,8192]{1,0:T(8,128)(2,1)S(1)}, bf16[16,8192]{1,0:T(8,128)(2,1)S(1)}, u32[]{:S(2)}, u32[]{:S(2)}) collective-permute-start(bf16[16,8192]{1,0:T(8,128)(2,1)S(1)} %get-tuple-element.318), channel_id=1, source_target_pairs={{0,16},{16,32},{32,48},{48,64},{64,80},{80,96},{96,112},{1,17},{17... | collective-permute-start | bytes 786440 | tf_op jit(solution)/shard_map/while/body/eval_jaxpr/ppermute | solution.py:14
  441.5 7.7 %collective-permute-start = (bf16[16,8192]{1,0:T(8,128)(2,1)S(1)}, bf16[16,8192]{1,0:T(8,128)(2,1)S(1)}, u32[]{:S(2)}, u32[]{:S(2)}) collective-permute-start(bf16[16,8192]{1,0:T(8,128)(2,1)S(1)} %get-tuple-element.318), channel_id=1, source_target_pairs={{0,16},{16,32},{32,48},{48,64},{64,80},{80,96},{96,112},{1,17},{17... | collective-permute-start | bytes 786440 | tf_op jit(solution)/shard_map/while/body/eval_jaxpr/ppermute | solution.py:14
  463.1 7.7 %collective-permute-start = (bf16[16,8192]{1,0:T(8,128)(2,1)S(1)}, bf16[16,8192]{1,0:T(8,128)(2,1)S(1)}, u32[]{:S(2)}, u32[]{:S(2)}) collective-permute-start(bf16[16,8192]{1,0:T(8,128)(2,1)S(1)} %get-tuple-element.318), channel_id=1, source_target_pairs={{0,16},{16,32},{32,48},{48,64},{64,80},{80,96},{96,112},{1,17},{17... | collective-permute-start | bytes 786440 | tf_op jit(solution)/shard_map/while/body/eval_jaxpr/ppermute | solution.py:14
  (23 other events, 22.6 us)
where the time goes:
time: 475 us; the launch traced here: 471 us
  waiting for transfers between devices  236 us (50%)
  local copies, waits for them, and re-layouts  90 us (19%)
  other arithmetic  58.2 us (12%)
  matrix products  50.3 us (11%)
  starting transfers between devices  35.6 us (7%)
    all_to_all x3, waiting for transfers between devices, on_device(): lax.all_to_all(sending, 'dp', split_axis=0, concat_axis=0, tiled=True)  179 us
    ppermute x10, waiting for transfers between devices, from_behind(): return lax.ppermute(block, axis, route)  57.6 us
    dot_general x10, matrix products, attend(): jnp.einsum('rkgl,rlkd->rkgd', weights, values, preferred_element_type=jnp...  34.3 us
    while x80, local copies, waits for them, and re-layouts  34.3 us
    dynamic_update_slice x10, other arithmetic, tick(): lax.dynamic_update_slice(record, jnp.where(valid, result[None], prior), (...  20 us
    ppermute x10, starting transfers between devices, from_behind(): return lax.ppermute(block, axis, route)  19.1 us
    squeeze x10, local copies, waits for them, and re-layouts, tick(): lax.dynamic_slice(states, (step, first, 0, 0), (1, requests, length, feat...  17.7 us
    all_to_all x3, starting transfers between devices, on_device(): lax.all_to_all(sending, 'dp', split_axis=0, concat_axis=0, tiled=True)  16.5 us
  transfers between devices with their start and end apart: 13, of which 13 were waited for; matrix products, arithmetic and copies ran while one was open for 1% of the time, Pallas kernels for 0%

commit v1 on v0

v1 whole, which is shorter than its diff:
```python
import functools

import jax
import jax.numpy as jnp
from jax import lax
from jax.experimental import pallas as pl
from jax.experimental.pallas import tpu as pltpu
from jax.sharding import PartitionSpec as P

HEADS = 64
KVH = 8
HD = 128
STEPS = 3
REQS = 16
BEAMS = 16
LEN = 32
PAST = LEN - STEPS
D = HEADS * HD
KV2 = 2 * KVH * HD
HALF = BEAMS // 2
EXTRA = 8
BF = jnp.bfloat16
F32 = jnp.float32
VMEM = pltpu.VMEM
SMEM = pltpu.SMEM


def spec(space):
    return pl.BlockSpec(memory_space=space)


def pack_kernel(which_ref, cache_ref, fresh_ref, rows_ref, out_ref, fresh, flat):
    del which_ref
    for u in range(STEPS):
        fresh[u * REQS : (u + 1) * REQS, :] = fresh_ref[u].astype(F32)
    for a in range(HEADS):
        tile = rows_ref[0, :, a * HD : (a + 1) * HD].astype(F32)
        flat[pl.ds(a, 8, stride=HEADS), :] = tile[:8]
        flat[pl.ds(8 * HEADS + a, 8, stride=HEADS), :] = tile[8:]
    place = lax.broadcasted_iota(jnp.int32, (16, KV2), 0)

    def one(r, _):
        out_ref[r, 0:16, :] = cache_ref[r, 0:16, :]
        late = cache_ref[r, 16:32, :].astype(F32)
        for u in range(STEPS):
            new = fresh[pl.ds(u * REQS + r, 1), :]
            late = jnp.where(place == PAST - 16 + u, new, late)
        out_ref[r, 16:32, :] = late.astype(BF)
        for k in range(8):
            part = flat[pl.ds(pl.multiple_of(r * HEADS + 8 * k, 8), 8), :]
            out_ref[r, LEN : LEN + EXTRA, k * HD : (k + 1) * HD] = part.astype(BF)
        return 0

    lax.fori_loop(0, REQS, one, 0)


def pack(which, slots, fresh, rows):
    return pl.pallas_call(
        pack_kernel,
        out_shape=jax.ShapeDtypeStruct((REQS, LEN + EXTRA, KV2), BF),
        grid_spec=pltpu.PrefetchScalarGridSpec(
            num_scalar_prefetch=1,
            grid=(1,),
            in_specs=[
                pl.BlockSpec((REQS, LEN, KV2), lambda i, w: (0, 0, 0)),
                pl.BlockSpec((STEPS, REQS, KV2), lambda i, w: (0, 0, 0)),
                pl.BlockSpec((1, REQS, D), lambda i, w: (w[0], 0, 0)),
            ],
            out_specs=pl.BlockSpec((REQS, LEN + EXTRA, KV2), lambda i, w: (0, 0, 0)),
            scratch_shapes=[VMEM((STEPS * REQS, KV2), F32), VMEM((REQS * HEADS, HD), F32)],
        ),
        compiler_params=pltpu.CompilerParams(vmem_limit_bytes=24 * 2**20),
        name="pack",
    )(which, slots, fresh, rows)


def first_kernel(idx_ref, extra_ref, out_ref, flat):
    core = idx_ref[1]
    for j in range(HALF):
        for k in range(8):
            part = extra_ref[HALF * core + j, :, k * HD : (k + 1) * HD].astype(F32)
            flat[j * HEADS + 8 * k : j * HEADS + 8 * k + 8, :] = part
    for a in range(HEADS):
        out_ref[:, a * HD : (a + 1) * HD] = flat[pl.ds(a, HALF, stride=HEADS), :].astype(BF)


def first_rows(idx, arrived):
    return pl.pallas_call(
        first_kernel,
        out_shape=jax.ShapeDtypeStruct((HALF, D), BF),
        grid=(1,),
        in_specs=[
            spec(SMEM),
            pl.BlockSpec((BEAMS, EXTRA, D // 8), lambda i: (0, LEN // EXTRA, 0)),
        ],
        out_specs=pl.BlockSpec((HALF, D), lambda i: (0, 0)),
        scratch_shapes=[VMEM((HALF * HEADS, HD), F32)],
        name="first_rows",
    )(idx, arrived)


def parent(par_ref, step, beam, mine):
    return par_ref[step * BEAMS * REQS + beam * REQS + mine]


def tick_kernel(tick, *refs):
    idx_ref, par_ref, gain_own, gain_oth, carry_ref, y_ref, yo_ref = refs[:7]
    refs = refs[7:] if tick == 0 else refs[9:]
    out_ref, r_own, r_oth, buf, bias, h, flat, sent, sems, osems = refs
    stage, core, mine = idx_ref[0], idx_ref[1], idx_ref[2]
    step = tick - stage
    active = (step >= 0) & (step < STEPS)

    @pl.when(jnp.logical_not(active))
    def _():
        out_ref[...] = carry_ref[...]

    @pl.when(active)
    def _():
        pltpu.make_async_copy(y_ref.at[:, pl.ds(0, LEN), :], buf.at[core], sems.at[core]).start()
        other = 1 - core
        pltpu.make_async_copy(yo_ref.at[:, pl.ds(0, LEN), :], buf.at[other], sems.at[other]).start()
        col = lax.broadcasted_iota(jnp.int32, (1, BEAMS * LEN), 1)
        beam, pos = col >> 5, col & (LEN - 1)
        for j in range(HALF):
            me = HALF * core + j
            c2 = jnp.where(step == 2, parent(par_ref, 2, me, mine), me)
            c1 = jnp.where(step >= 1, parent(par_ref, 1, c2, mine), c2)
            root = parent(par_ref, 0, c1, mine)
            second = jnp.where(step >= 1, c2, -1)
            third = jnp.where(step == 2, me, -1)
            want = jnp.where(
                pos < PAST,
                root,
                jnp.where(pos == PAST, c1, jnp.where(pos == PAST + 1, second, third)),
            )
            bias[j : j + 1, :] = jnp.where(beam == want, 0.0, -1e30)
        h[...] = carry_ref[...].astype(F32)
        for layer in range(2):
            pltpu.make_async_copy(
                y_ref.at[:, pl.ds(0, LEN), :], buf.at[layer], sems.at[layer]
            ).wait()
            x = h[...]
            scale = lax.rsqrt(jnp.sum(x * x, axis=1, keepdims=True) * (1.0 / D) + 1e-05)
            pick = jnp.full((1, HD), core, jnp.int32) == layer
            for g in range(KVH):
                heads = [
                    slice((g * KVH + a) * HD, (g * KVH + a + 1) * HD) for a in range(HEADS // KVH)
                ]
                query = jnp.concatenate(
                    [
                        h[:, s]
                        * scale
                        * jnp.where(pick, gain_own[:, s].astype(F32), gain_oth[:, s].astype(F32))
                        for s in heads
                    ],
                    axis=0,
                ).astype(BF)
                keys = buf[layer, :, :, g * HD : (g + 1) * HD].reshape(BEAMS * LEN, HD)
                values = buf[layer, :, :, (KVH + g) * HD : (KVH + g + 1) * HD].reshape(
                    BEAMS * LEN, HD
                )
                scores = lax.dot_general(
                    query, keys, (((1,), (1,)), ((), ())), preferred_element_type=F32
                )
                scores = scores.reshape(HEADS // KVH, HALF, BEAMS * LEN) * HD ** (-0.5)
                scores = scores + bias[...][None]
                top = jnp.max(scores, axis=-1, keepdims=True)
                expo = jnp.exp(scores - top)
                weights = expo * (1.0 / jnp.sum(expo, axis=-1, keepdims=True))
                weights = weights.reshape(HEADS, BEAMS * LEN).astype(BF)
                attended = jnp.dot(weights, values, preferred_element_type=F32)
                for a, s in enumerate(heads):
                    total = (h[:, s] + attended[a * HALF : (a + 1) * HALF]).astype(BF)
                    h[:, s] = total.astype(F32)
                    flat[pl.ds(g * KVH + a, HALF, stride=HEADS), :] = total.astype(F32)
            sent[layer] = flat[...].astype(BF).reshape(HALF, HEADS, HD)

            @pl.when(core == layer)
            def _():
                pltpu.make_async_copy(sent.at[layer], r_own.at[:, step], osems.at[layer]).start()

            @pl.when(core != layer)
            def _():
                pltpu.make_async_copy(sent.at[layer], r_oth.at[:, step], osems.at[layer]).start()

        out_ref[...] = h[...].astype(BF)
        for layer in range(2):
            pltpu.make_async_copy(sent.at[layer], r_own.at[:, step], osems.at[layer]).wait()


def run_tick(tick, idx, par, gain_own, gain_oth, carry, y, yo, records):
    record = jax.ShapeDtypeStruct((HALF, STEPS, HEADS, HD), BF)
    return pl.pallas_call(
        functools.partial(tick_kernel, tick),
        out_shape=(jax.ShapeDtypeStruct((HALF, D), BF), record, record),
        in_specs=[spec(SMEM), spec(SMEM), spec(VMEM), spec(VMEM), spec(VMEM)]
        + [spec(pl.ANY)] * (2 + len(records)),
        out_specs=(spec(VMEM), spec(pl.ANY), spec(pl.ANY)),
        scratch_shapes=[
            VMEM((2, BEAMS, LEN, KV2), BF),
            VMEM((HALF, BEAMS * LEN), F32),
            VMEM((HALF, D), F32),
            VMEM((HALF * HEADS, HD), F32),
            VMEM((2, HALF, HEADS, HD), BF),
            pltpu.SemaphoreType.DMA((2,)),
            pltpu.SemaphoreType.DMA((2,)),
        ],
        input_output_aliases={7: 1, 8: 2} if records else {},
        compiler_params=pltpu.CompilerParams(vmem_limit_bytes=24 * 2**20),
        cost_estimate=pl.CostEstimate(flops=10**8, bytes_accessed=5 * 2**20, transcendentals=0),
        name="tick",
    )(idx, par, gain_own, gain_oth, carry, y, yo, *records)


GROUP = 4


def reorder_kernel(idx_ref, par_ref, y_ref, out_ref):
    mine = idx_ref[2]
    place = lax.broadcasted_iota(jnp.int32, (16, KV2), 0)

    def one(i, _):
        j = pl.program_id(0) * GROUP + i
        c2 = parent(par_ref, 2, j, mine)
        c1 = parent(par_ref, 1, c2, mine)
        root = parent(par_ref, 0, c1, mine)
        out_ref[i, 0:16, :] = y_ref[root, 0:16, :]
        late = y_ref[root, 16:32, :].astype(F32)
        for u, source in enumerate((c1, c2, j)):
            late = jnp.where(place == PAST - 16 + u, y_ref[source, 16:32, :].astype(F32), late)
        out_ref[i, 16:32, :] = late.astype(BF)
        return 0

    lax.fori_loop(0, GROUP, one, 0)


def reorder(idx, par, y):
    return pl.pallas_call(
        reorder_kernel,
        out_shape=jax.ShapeDtypeStruct((BEAMS, LEN, KV2), BF),
        grid=(BEAMS // GROUP,),
        in_specs=[
            spec(SMEM),
            spec(SMEM),
            pl.BlockSpec((BEAMS, LEN + EXTRA, KV2), lambda i: (0, 0, 0)),
        ],
        out_specs=pl.BlockSpec((GROUP, LEN, KV2), lambda i: (i, 0, 0)),
        compiler_params=pltpu.CompilerParams(vmem_limit_bytes=24 * 2**20),
        cost_estimate=pl.CostEstimate(flops=10**6, bytes_accessed=5 * 2**20, transcendentals=0),
        name="reorder",
    )(idx, par, y)


def spread_kernel(in_ref, out_ref, flat):
    for r in range(REQS):
        flat[r * HEADS : (r + 1) * HEADS, :] = in_ref[r, 0].astype(F32)
    for a in range(HEADS):
        low = flat[pl.ds(a, 8, stride=HEADS), :]
        high = flat[pl.ds(8 * HEADS + a, 8, stride=HEADS), :]
        out_ref[0, :, a * HD : (a + 1) * HD] = jnp.concatenate([low, high], axis=0).astype(BF)


def spread(arrived):
    return pl.pallas_call(
        spread_kernel,
        out_shape=jax.ShapeDtypeStruct((STEPS, REQS, D), BF),
        grid=(STEPS,),
        in_specs=[pl.BlockSpec((REQS, 1, HEADS, HD), lambda t: (0, t, 0, 0))],
        out_specs=pl.BlockSpec((1, REQS, D), lambda t: (t, 0, 0)),
        scratch_shapes=[VMEM((REQS * HEADS, HD), F32)],
        name="spread",
    )(arrived)


def on_device(step_rows, cache, new_kv, gains, parents):
    sections = lax.axis_size("section")
    section = lax.axis_index("section")
    stage, core = section // 2, section % 2
    swap = [(i, i ^ 1) for i in range(sections)]
    ahead = [(i, (i + 2) % sections) for i in range(sections)]
    idx = jnp.stack([stage, core, lax.axis_index("dp")]).astype(jnp.int32)
    par = parents.reshape(-1)
    which = jnp.minimum((sections // 2 - stage) % (sections // 2), STEPS - 1)
    which = which.astype(jnp.int32).reshape(1)
    gain_own = gains
    gain_oth = lax.ppermute(gains, "section", swap)

    packed = pack(which, cache[0, :, 0], new_kv[0, :, :, 0], step_rows[:, :, 0])
    y = lax.all_to_all(packed, "dp", split_axis=0, concat_axis=0, tiled=True)
    yo = lax.ppermute(y, "section", swap)
    carry = first_rows(idx, y)
    back = reorder(idx, par, y)
    cache_out = lax.all_to_all(back, "dp", split_axis=0, concat_axis=0, tiled=True)

    records = ()
    ticks = STEPS + sections // 2 - 1
    for tick in range(ticks):
        carry, *records = run_tick(tick, idx, par, gain_own, gain_oth, carry, y, yo, records)
        if tick < ticks - 1:
            carry = lax.ppermute(carry, "section", ahead)
    own, oth = records
    oth = lax.ppermute(oth, "section", swap)
    rows = jnp.where(
        core == 0, jnp.concatenate([own, oth], axis=0), jnp.concatenate([oth, own], axis=0)
    )
    rows = lax.all_to_all(rows, "dp", split_axis=0, concat_axis=0, tiled=True)
    rows = spread(rows)
    return (rows[None, :, :, None], cache_out[None, :, None])


def solution(mesh):
    return jax.shard_map(
        on_device,
        mesh=mesh,
        in_specs=(
            P(None, None, "dp", None),
            P("section", None, "dp", None, None),
            P("section", None, None, "dp", None),
            P("section", None),
            P(),
        ),
        out_specs=(P("section", None, None, "dp", None), P("section", None, "dp", None, None)),
        check_vma=False,
    )
```

time: 475 us -> 163 us (0.34)
  waiting for transfers between devices: 236 us -> 34.5 us
  local copies, waits for them, and re-layouts: 90 us -> 12.3 us
  other arithmetic: 58.2 us -> 1.78 us
  matrix products: 50.3 us -> 0 us
  blocking collectives: 0 us -> 40.8 us
  Pallas kernels: 0 us -> 30.6 us
  starting transfers between devices: 35.6 us -> 41.6 us
    all_to_all x3 -> x2, waiting for transfers between devices: 179 us -> 14.9 us  [the longest x1 14.9 us: on_device(): rows = lax.all_to_all(rows, 'dp', split_axis=0, concat_axis=0, tiled=True)]
    dot_general x20 -> x0, matrix products: 50.3 us -> none  [the longest x10 34.3 us: attend(): jnp.einsum('rkgl,rlkd->rkgd', weights, values, preferred_element_type=jnp...]
    all_to_all x0 -> x1, blocking collectives: none -> 40.8 us  [on_device(): y = lax.all_to_all(packed, 'dp', split_axis=0, concat_axis=0, tiled=True)]
    ppermute x10 -> x8, waiting for transfers between devices: 57.6 us -> 19.6 us  [the longest x5 18.3 us: on_device(): carry = lax.ppermute(carry, 'section', ahead)]
    while x80 -> x0, local copies, waits for them, and re-layouts: 34.3 us -> none
    pallas_call x0 -> x10, Pallas kernels: none -> 30.6 us  [the longest x6 23.2 us: run_tick(): pl.pallas_call(functools.partial(tick_kernel, tick), out_shape=(jax.Shape...]
    gather x6 -> x0, local copies, waits for them, and re-layouts: 24 us -> none  [the longest x3 12.6 us: place_arrived(): return flat[sources * capacity + slot_rank]]
    dynamic_update_slice x10 -> x0, other arithmetic: 20 us -> none  [tick(): lax.dynamic_update_slice(record, jnp.where(valid, result[None], prior), (...]
  transfers between devices with their start and end apart: 13 -> 10, of which waited for: 13 -> 7; matrix products, arithmetic and copies ran while one was open for 1% -> 1% of each run, Pallas kernels for 0% -> 16%
where the time goes in v1:
time: 163 us; the launch traced here: 162 us
  starting transfers between devices  41.6 us (26%)
  blocking collectives  40.8 us (25%)
  waiting for transfers between devices  34.5 us (21%)
  Pallas kernels  30.6 us (19%)
  local copies, waits for them, and re-layouts  12.3 us (8%)
  other arithmetic  1.78 us (1%)
    all_to_all x1, blocking collectives, on_device(): y = lax.all_to_all(packed, 'dp', split_axis=0, concat_axis=0, tiled=True)  40.8 us
    ppermute x5, starting transfers between devices, on_device(): carry = lax.ppermute(carry, 'section', ahead)  25.5 us
    pallas_call x6, Pallas kernels, run_tick(): pl.pallas_call(functools.partial(tick_kernel, tick), out_shape=(jax.Shape...  23.2 us
    ppermute x5, waiting for transfers between devices, on_device(): carry = lax.ppermute(carry, 'section', ahead)  18.3 us
    all_to_all x1, waiting for transfers between devices, on_device(): rows = lax.all_to_all(rows, 'dp', split_axis=0, concat_axis=0, tiled=True)  14.9 us
    unnamed x26, local copies, waits for them, and re-layouts  12.2 us
    all_to_all x1, starting transfers between devices, on_device(): rows = lax.all_to_all(rows, 'dp', split_axis=0, concat_axis=0, tiled=True)  6.37 us
    ppermute x1, starting transfers between devices, on_device(): oth = lax.ppermute(oth, 'section', swap)  4.72 us
  transfers between devices with their start and end apart: 10, of which 7 were waited for; matrix products, arithmetic and copies ran while one was open for 1% of the time, Pallas kernels for 16%

profile of v1, /device:TPU:96, one launch (start us, length us, event | category | flops | bytes accessed | tf_op | source)
XLA Modules:
  0.0 162.5 jit_solution(16019920809488735680)
XLA Ops:
  0.7 1.6 copy-done.3
  5.2 40.8 %all_to_all.15.extra_ref.refs_5_.y_ref = bf16[16,40,2048]{2,1,0:T(8,128)(2,1)S(1)} all-to-all(bf16[16,40,2048]{2,1,0:T(8,128)(2,1)S(1)} %pack.1), channel_id=1, replica_groups=mesh['section'=8,'dp'=16] {'dp'}, dimensions={0} | all-to-all | bytes 5242880 | tf_op jit(solution)/shard_map/all_to_all | solution.py:290
  47.5 1.3 reorder.1
  48.8 1.3 copy-done.2
  50.1 4.6 %all-to-all-start.2 = ((bf16[16,32,2048]{2,1,0:T(8,128)(2,1)}), bf16[16,32,2048]{2,1,0:T(8,128)(2,1)}, u32[]{:S(2)}, u32[]{:S(2)}) async-start(bf16[16,32,2048]{2,1,0:T(8,128)(2,1)} %copy-done.2), calls=%async_computation.2 | async-start | bytes 4194304 | tf_op jit(solution)/shard_map/all_to_all | solution.py:294
  55.2 1.8 %first_rows.1.refs_4_ = bf16[8,8192]{1,0:T(8,128)(2,1)} custom-call(s32[3]{0:T(128)} %copy-done.8, bf16[16,40,2048]{2,1,0:T(8,128)(2,1)} %copy-done), custom_call_target="tpu_custom_call" | custom-call | tf_op jit(solution)/shard_map/first_rows/pallas_call | solution.py:88
  57.1 1.7 %copy-done.1 = bf16[16,40,2048]{2,1,0:T(8,128)(2,1)S(1)} copy-done((bf16[16,40,2048]{2,1,0:T(8,128)(2,1)S(1)}, bf16[16,40,2048]{2,1,0:T(8,128)(2,1)}, u32[]{:S(2)}) %copy-start.1) | copy-done | bytes 2621464
  60.3 5.5 %collective-permute-start.2 = (bf16[8,8192]{1,0:T(8,128)(2,1)S(1)}, bf16[8,8192]{1,0:T(8,128)(2,1)S(1)}, u32[]{:S(2)}, u32[]{:S(2)}) collective-permute-start(bf16[8,8192]{1,0:T(8,128)(2,1)S(1)} %get-tuple-element.19), channel_id=1, source_target_pairs={{0,32},{16,48},{32,64},{48,80},{64,96},{80,112},{96,0},{112,16},{1... | collective-permute-start | bytes 393224 | tf_op jit(solution)/shard_map/ppermute | solution.py:301
  65.8 3.3 %collective-permute-done.2.refs_4_ = bf16[8,8192]{1,0:T(8,128)(2,1)S(1)} collective-permute-done((bf16[8,8192]{1,0:T(8,128)(2,1)S(1)}, bf16[8,8192]{1,0:T(8,128)(2,1)S(1)}, u32[]{:S(2)}, u32[]{:S(2)}) %collective-permute-start.2) | collective-permute-done | bytes 131104 | tf_op jit(solution)/shard_map/ppermute | solution.py:301
  69.8 9.9 %collective-permute-start.3 = (bf16[8,8192]{1,0:T(8,128)(2,1)S(1)}, bf16[8,8192]{1,0:T(8,128)(2,1)S(1)}, u32[]{:S(2)}, u32[]{:S(2)}) collective-permute-start(bf16[8,8192]{1,0:T(8,128)(2,1)S(1)} %get-tuple-element.22), channel_id=1, source_target_pairs={{0,32},{16,48},{32,64},{48,80},{64,96},{80,112},{96,0},{112,16},{1... | collective-permute-start | bytes 393224 | tf_op jit(solution)/shard_map/ppermute | solution.py:301
  79.7 2.5 %collective-permute-done.3.refs_4_ = bf16[8,8192]{1,0:T(8,128)(2,1)S(1)} collective-permute-done((bf16[8,8192]{1,0:T(8,128)(2,1)S(1)}, bf16[8,8192]{1,0:T(8,128)(2,1)S(1)}, u32[]{:S(2)}, u32[]{:S(2)}) %collective-permute-start.3) | collective-permute-done | bytes 131104 | tf_op jit(solution)/shard_map/ppermute | solution.py:301
  82.9 9.9 %collective-permute-start.4 = (bf16[8,8192]{1,0:T(8,128)(2,1)S(1)}, bf16[8,8192]{1,0:T(8,128)(2,1)S(1)}, u32[]{:S(2)}, u32[]{:S(2)}) collective-permute-start(bf16[8,8192]{1,0:T(8,128)(2,1)S(1)} %get-tuple-element.25), channel_id=1, source_target_pairs={{0,32},{16,48},{32,64},{48,80},{64,96},{80,112},{96,0},{112,16},{1... | collective-permute-start | bytes 393224 | tf_op jit(solution)/shard_map/ppermute | solution.py:301
  92.8 2.5 %collective-permute-done.4.refs_4_ = bf16[8,8192]{1,0:T(8,128)(2,1)S(1)} collective-permute-done((bf16[8,8192]{1,0:T(8,128)(2,1)S(1)}, bf16[8,8192]{1,0:T(8,128)(2,1)S(1)}, u32[]{:S(2)}, u32[]{:S(2)}) %collective-permute-start.4) | collective-permute-done | bytes 131104 | tf_op jit(solution)/shard_map/ppermute | solution.py:301
  95.3 7.0 %tick.9 = (bf16[8,8192]{1,0:T(8,128)(2,1)S(1)}, bf16[8,3,64,128]{3,2,1,0:T(8,128)(2,1)S(1)}, bf16[8,3,64,128]{3,2,1,0:T(8,128)(2,1)S(1)}) custom-call(s32[3]{0:T(128)S(1)} %copy-done.9, s32[768]{0:T(1024)S(1)} %reshape.10.refs_1_.par_ref, bf16[1,8192]{1,0:T(2,128)(2,1)S(1)} %copy-done.4, ...), custom_call_target="tpu_custom_call", output_to_operand_aliasing={{1}: (7, {}), {2}: (8, {})} | custom-call | flops 100000000 | bytes 5242880 | tf_op jit(solution)/shard_map/tick/pallas_call | solution.py:194
  102.4 5.0 %collective-permute-done.5.refs_4_ = bf16[8,8192]{1,0:T(8,128)(2,1)S(1)} collective-permute-done((bf16[8,8192]{1,0:T(8,128)(2,1)S(1)}, bf16[8,8192]{1,0:T(8,128)(2,1)S(1)}, u32[]{:S(2)}, u32[]{:S(2)}) %collective-permute-start.5) | collective-permute-done | bytes 131104 | tf_op jit(solution)/shard_map/ppermute | solution.py:301
  107.4 6.8 %tick.10 = (bf16[8,8192]{1,0:T(8,128)(2,1)S(1)}, bf16[8,3,64,128]{3,2,1,0:T(8,128)(2,1)S(1)}, bf16[8,3,64,128]{3,2,1,0:T(8,128)(2,1)S(1)}) custom-call(s32[3]{0:T(128)S(1)} %copy-done.9, s32[768]{0:T(1024)S(1)} %reshape.10.refs_1_.par_ref, bf16[1,8192]{1,0:T(2,128)(2,1)S(1)} %copy-done.4, ...), custom_call_target="tpu_custom_call", output_to_operand_aliasing={{1}: (7, {}), {2}: (8, {})} | custom-call | flops 100000000 | bytes 5242880 | tf_op jit(solution)/shard_map/tick/pallas_call | solution.py:194
  114.3 5.0 %collective-permute-done.6.refs_4_ = bf16[8,8192]{1,0:T(8,128)(2,1)S(1)} collective-permute-done((bf16[8,8192]{1,0:T(8,128)(2,1)S(1)}, bf16[8,8192]{1,0:T(8,128)(2,1)S(1)}, u32[]{:S(2)}, u32[]{:S(2)}) %collective-permute-start.6) | collective-permute-done | bytes 131104 | tf_op jit(solution)/shard_map/ppermute | solution.py:301
  119.2 7.5 %tick.11 = (bf16[8,8192]{1,0:T(8,128)(2,1)}, bf16[8,3,64,128]{3,2,1,0:T(8,128)(2,1)S(1)}, bf16[8,3,64,128]{3,2,1,0:T(8,128)(2,1)S(1)}) custom-call(s32[3]{0:T(128)S(1)} %copy-done.9, s32[768]{0:T(1024)S(1)} %reshape.10.refs_1_.par_ref, bf16[1,8192]{1,0:T(2,128)(2,1)S(1)} %copy-done.4, ...), custom_call_target="tpu_custom_call", output_to_operand_aliasing={{1}: (7, {}), {2}: (8, {})} | custom-call | flops 100000000 | bytes 5242880 | tf_op jit(solution)/shard_map/tick/pallas_call | solution.py:194
  126.7 4.7 %collective-permute-start.7 = (bf16[8,3,64,128]{3,2,1,0:T(8,128)(2,1)S(1)}, bf16[8,3,64,128]{3,2,1,0:T(8,128)(2,1)S(1)}, u32[]{:S(2)}, u32[]{:S(2)}) collective-permute-start(bf16[8,3,64,128]{3,2,1,0:T(8,128)(2,1)S(1)} %get-tuple-element.35), channel_id=1, source_target_pairs={{0,16},{16,0},{32,48},{48,32},{64,80},{80,64},{96,112},{112,96},{1... | collective-permute-start | bytes 1179656 | tf_op jit(solution)/shard_map/ppermute | solution.py:303
  131.4 1.3 collective-permute-done.7
  133.8 6.4 %all-to-all-start.1 = ((bf16[16,3,64,128]{3,2,1,0:T(8,128)(2,1)}), bf16[16,3,64,128]{3,2,1,0:T(8,128)(2,1)S(1)}, u32[]{:S(2)}, u32[]{:S(2)}) async-start(bf16[16,3,64,128]{3,2,1,0:T(8,128)(2,1)} %maximum_select_fusion), calls=%async_computation.1 | async-start | bytes 1572864 | tf_op jit(solution)/shard_map/all_to_all | solution.py:307
  140.2 14.9 %all-to-all-done.1.in_ref = bf16[16,3,64,128]{3,2,1,0:T(8,128)(2,1)S(1)} async-done(((bf16[16,3,64,128]{3,2,1,0:T(8,128)(2,1)}), bf16[16,3,64,128]{3,2,1,0:T(8,128)(2,1)S(1)}, u32[]{:S(2)}, u32[]{:S(2)}) %all-to-all-start.1) | async-done | bytes 786464 | tf_op jit(solution)/shard_map/all_to_all | solution.py:307
  155.9 3.4 %spread.1 = bf16[3,16,8192]{2,1,0:T(8,128)(2,1)} custom-call(bf16[16,3,64,128]{3,2,1,0:T(8,128)(2,1)} %copy-done.10), custom_call_target="tpu_custom_call" | custom-call | tf_op jit(solution)/shard_map/spread/pallas_call | solution.py:265
  159.3 3.2 %copy.30 = bf16[1,16,1,32,2048]{4,3,2,1,0:T(8,128)(2,1)} copy(bf16[1,16,1,32,2048]{4,3,2,1,0:T(8,128)(2,1)} %bitcast.10) | data formatting | bytes 4194304
  (37 shorter events, 9.8 us)
Async XLA Ops:
  0.7 1.6 copy-start.3
  2.3 1.1 copy-start.5
  3.4 0.9 copy-start.7
  5.2 41.4 %copy-start.11 = (s32[3,16,16,1]{2,3,1,0:T(1,128)S(1)}, s32[3,16,16,1]{2,3,1,0:T(1,128)}, u32[]{:S(2)}) copy-start(s32[3,16,16,1]{2,3,1,0:T(1,128)} %param.9) | copy-start | bytes 9220
  46.1 9.2 %copy-start = (bf16[16,40,2048]{2,1,0:T(8,128)(2,1)}, bf16[16,40,2048]{2,1,0:T(8,128)(2,1)S(1)}, u32[]{:S(2)}) copy-start(bf16[16,40,2048]{2,1,0:T(8,128)(2,1)S(1)} %all_to_all.15.extra_ref.refs_5_.y_ref) | copy-start | bytes 7864324
  46.1 11.0 %collective-permute-start.1 = (bf16[16,40,2048]{2,1,0:T(8,128)(2,1)S(1)}, bf16[16,40,2048]{2,1,0:T(8,128)(2,1)}, u32[]{:S(2)}, u32[]{:S(2)}) collective-permute-start(bf16[16,40,2048]{2,1,0:T(8,128)(2,1)S(1)} %all_to_all.15.extra_ref.refs_5_.y_ref), channel_id=1, source_target_pairs={{0,16},{16,0},{32,48},{48,32},{64,80},{80,64},{96,112},{112,96},{1... | collective-permute-start | bytes 7864328 | tf_op jit(solution)/shard_map/ppermute | solution.py:291
  47.5 1.3 copy-start.8
  48.8 1.3 copy-start.2
  50.1 4.6 %copy-start.4 = (bf16[1,8192]{1,0:T(2,128)(2,1)S(1)}, bf16[1,8192]{1,0:T(2,128)(2,1)}, u32[]{:S(2)}) copy-start(bf16[1,8192]{1,0:T(2,128)(2,1)} %refs_2_.11) | copy-start | bytes 49156
  50.1 83.7 %all-to-all-start.2 = ((bf16[16,32,2048]{2,1,0:T(8,128)(2,1)}), bf16[16,32,2048]{2,1,0:T(8,128)(2,1)}, u32[]{:S(2)}, u32[]{:S(2)}) async-start(bf16[16,32,2048]{2,1,0:T(8,128)(2,1)} %copy-done.2), calls=%async_computation.2 | async-start | bytes 4194304 | tf_op jit(solution)/shard_map/all_to_all | solution.py:294
  54.7 2.3 %copy-start.9 = (s32[3]{0:T(128)S(1)}, s32[3]{0:T(128)}, u32[]{:S(2)}) copy-start(s32[3]{0:T(128)} %copy-done.8) | copy-start | bytes 40
  54.7 2.3 %collective-permute-start = (bf16[1,8192]{1,0:T(2,128)(2,1)S(1)}, bf16[1,8192]{1,0:T(2,128)(2,1)S(1)}, u32[]{:S(2)}, u32[]{:S(2)}) collective-permute-start(bf16[1,8192]{1,0:T(2,128)(2,1)S(1)} %copy-done.4), channel_id=1, source_target_pairs={{0,16},{16,0},{32,48},{48,32},{64,80},{80,64},{96,112},{112,96},{1... | collective-permute-start | bytes 49160 | tf_op jit(solution)/shard_map/ppermute | solution.py:287
  57.0 1.7 %copy-start.1 = (bf16[16,40,2048]{2,1,0:T(8,128)(2,1)S(1)}, bf16[16,40,2048]{2,1,0:T(8,128)(2,1)}, u32[]{:S(2)}) copy-start(bf16[16,40,2048]{2,1,0:T(8,128)(2,1)} %copy-done) | copy-start | bytes 7864324
  58.8 0.9 copy-start.6
  60.3 8.8 %collective-permute-start.2 = (bf16[8,8192]{1,0:T(8,128)(2,1)S(1)}, bf16[8,8192]{1,0:T(8,128)(2,1)S(1)}, u32[]{:S(2)}, u32[]{:S(2)}) collective-permute-start(bf16[8,8192]{1,0:T(8,128)(2,1)S(1)} %get-tuple-element.19), channel_id=1, source_target_pairs={{0,32},{16,48},{32,64},{48,80},{64,96},{80,112},{96,0},{112,16},{1... | collective-permute-start | bytes 393224 | tf_op jit(solution)/shard_map/ppermute | solution.py:301
  69.8 12.5 %collective-permute-start.3 = (bf16[8,8192]{1,0:T(8,128)(2,1)S(1)}, bf16[8,8192]{1,0:T(8,128)(2,1)S(1)}, u32[]{:S(2)}, u32[]{:S(2)}) collective-permute-start(bf16[8,8192]{1,0:T(8,128)(2,1)S(1)} %get-tuple-element.22), channel_id=1, source_target_pairs={{0,32},{16,48},{32,64},{48,80},{64,96},{80,112},{96,0},{112,16},{1... | collective-permute-start | bytes 393224 | tf_op jit(solution)/shard_map/ppermute | solution.py:301
  82.9 12.4 %collective-permute-start.4 = (bf16[8,8192]{1,0:T(8,128)(2,1)S(1)}, bf16[8,8192]{1,0:T(8,128)(2,1)S(1)}, u32[]{:S(2)}, u32[]{:S(2)}) collective-permute-start(bf16[8,8192]{1,0:T(8,128)(2,1)S(1)} %get-tuple-element.25), channel_id=1, source_target_pairs={{0,32},{16,48},{32,64},{48,80},{64,96},{80,112},{96,0},{112,16},{1... | collective-permute-start | bytes 393224 | tf_op jit(solution)/shard_map/ppermute | solution.py:301
  102.3 5.0 %collective-permute-start.5 = (bf16[8,8192]{1,0:T(8,128)(2,1)S(1)}, bf16[8,8192]{1,0:T(8,128)(2,1)S(1)}, u32[]{:S(2)}, u32[]{:S(2)}) collective-permute-start(bf16[8,8192]{1,0:T(8,128)(2,1)S(1)} %get-tuple-element.28), channel_id=1, source_target_pairs={{0,32},{16,48},{32,64},{48,80},{64,96},{80,112},{96,0},{112,16},{1... | collective-permute-start | bytes 393224 | tf_op jit(solution)/shard_map/ppermute | solution.py:301
  114.2 5.0 %collective-permute-start.6 = (bf16[8,8192]{1,0:T(8,128)(2,1)S(1)}, bf16[8,8192]{1,0:T(8,128)(2,1)S(1)}, u32[]{:S(2)}, u32[]{:S(2)}) collective-permute-start(bf16[8,8192]{1,0:T(8,128)(2,1)S(1)} %get-tuple-element.31), channel_id=1, source_target_pairs={{0,32},{16,48},{32,64},{48,80},{64,96},{80,112},{96,0},{112,16},{1... | collective-permute-start | bytes 393224 | tf_op jit(solution)/shard_map/ppermute | solution.py:301
  126.7 6.1 %collective-permute-start.7 = (bf16[8,3,64,128]{3,2,1,0:T(8,128)(2,1)S(1)}, bf16[8,3,64,128]{3,2,1,0:T(8,128)(2,1)S(1)}, u32[]{:S(2)}, u32[]{:S(2)}) collective-permute-start(bf16[8,3,64,128]{3,2,1,0:T(8,128)(2,1)S(1)} %get-tuple-element.35), channel_id=1, source_target_pairs={{0,16},{16,0},{32,48},{48,32},{64,80},{80,64},{96,112},{112,96},{1... | collective-permute-start | bytes 1179656 | tf_op jit(solution)/shard_map/ppermute | solution.py:303
  133.8 21.2 %all-to-all-start.1 = ((bf16[16,3,64,128]{3,2,1,0:T(8,128)(2,1)}), bf16[16,3,64,128]{3,2,1,0:T(8,128)(2,1)S(1)}, u32[]{:S(2)}, u32[]{:S(2)}) async-start(bf16[16,3,64,128]{3,2,1,0:T(8,128)(2,1)} %maximum_select_fusion), calls=%async_computation.1 | async-start | bytes 1572864 | tf_op jit(solution)/shard_map/all_to_all | solution.py:307
  155.0 0.9 copy-start.10
